TPU v7x, 128 devices: a whole 4x4x4 slice. The times are simulated.
128 devices in a mesh: seq: 8 (over y_hi, x), rep: 16 (over y_lo, z, core).
Axes of the slice: x: 4, y: 4 (y_hi: 2, y_lo: 2; y = y_hi * 2 + y_lo), z: 4, core: 2. Of those that a mesh axis runs over, the one named last changes fastest.
Arguments:
- inputs: bfloat16 [16, 8192, 768], P('rep', 'seq'), may hold values from -6 to 6
- trunk_grad: bfloat16 [16, 4096, 1536], P('rep', None, 'seq'), may hold values from -6 to 6
- weights: bfloat16 [5, 768, 1536], P(None, 'rep', 'seq'), may hold values from -0.09375 to 0.09375
Outputs:
- input_grad: bfloat16 [16, 8192, 768], P('rep', 'seq')
- weight_grad: float32 [5, 768, 1536], P(None, 'rep', 'seq')
All inputs are finite; a program needn't handle non-finite values.
Results may differ from a plain program's by a relative error of at most 0.0027.
Values may be sent and summed in bfloat16 or wider, within the bound.
A program may use at most 192 MiB of HBM per device.

v0:
```python
import jax
import jax.numpy as jnp
from jax import lax
from jax.sharding import PartitionSpec as P


def with_halo(value, sides, width):
    for axis, dim in sides:
        peers, length = (lax.axis_size(axis), value.shape[dim])
        up = [(i, (i + 1) % peers) for i in range(peers - 1)]
        down = [(j, i) for i, j in up]
        last = lax.slice_in_dim(value, length - width, length, axis=dim)
        leading = lax.slice_in_dim(value, 0, width, axis=dim)
        before = lax.ppermute(last, axis, up)
        after = lax.ppermute(leading, axis, down)
        value = jnp.concatenate([before, value, after], axis=dim)
    return value


def contract_last(left, right):
    return lax.dot_general(
        left, right, (((1,), (1,)), ((), ())), preferred_element_type=jnp.float32
    )


def contract_first(left, right):
    return lax.dot_general(
        left, right, (((0,), (0,)), ((), ())), preferred_element_type=jnp.float32
    )


def on_device(inputs, trunk_grad, weights):
    taps = weights.shape[0]
    grad = lax.all_to_all(trunk_grad, "seq", split_axis=1, concat_axis=2, tiled=True)
    grad_up = jnp.repeat(grad.astype(jnp.float32) * 0.5, 2, axis=1).astype(jnp.bfloat16)
    rows = grad_up.shape[1]
    padded = with_halo(grad_up, (("seq", 1),), 2)
    shifts = [padded[0, 4 - k : 4 - k + rows] for k in range(taps)]
    inputs_f = inputs[0].astype(jnp.float32)
    act_vals, back = jax.vjp(jax.nn.gelu, inputs_f)
    slope = back(jnp.ones_like(inputs_f))[0]
    act = act_vals.astype(jnp.bfloat16)
    in_width = inputs.shape[2]
    columns = lax.all_gather(weights, "seq", axis=2, tiled=True)
    piece = lax.all_gather(columns, "rep", axis=1, tiled=True)
    result = contract_last(shifts[0], piece[0])
    for project_k in range(1, taps):
        result = result + contract_last(shifts[project_k], piece[project_k])
    input_grad = (result * slope + grad_up[0, :, :in_width].astype(jnp.float32)).astype(
        jnp.bfloat16
    )
    scale_factor = float(rows * lax.axis_size("seq") * lax.axis_size("rep")) ** (-0.5)
    terms = jnp.stack([contract_first(act, shifts[k]) for k in range(taps)]) * scale_factor
    partial_sum = lax.psum_scatter(terms, "rep", scatter_dimension=1, tiled=True)
    weight_grad = lax.psum_scatter(partial_sum, "seq", scatter_dimension=2, tiled=True)
    return (input_grad[None], weight_grad)


def solution(mesh):
    in_specs = (P("rep", "seq", None), P("rep", None, "seq"), P(None, "rep", "seq"))
    out_specs = (P("rep", "seq", None), P(None, "rep", "seq"))
    return jax.shard_map(
        on_device, mesh=mesh, in_specs=in_specs, out_specs=out_specs, check_vma=False
    )
```

profile of v0, /device:TPU:0, one launch (start us, length us, event | category | flops | bytes accessed | tf_op | source)
XLA Modules:
  0.0 423.1 jit_solution(8136104448469468959)
XLA Ops:
  8.4 44.7 %all_gather.6 = bf16[5,48,1536]{1,0,2:T(8,128)(2,1)S(1)} all-gather(bf16[5,48,192]{1,0,2:T(8,128)(2,1)S(1)} %copy.23), channel_id=1, replica_groups=mesh['seq'=8,'rep'=16] {'seq'}, dimensions={2}, use_global_device_ids=true | all-gather | bytes 829440 | tf_op jit(solution)/shard_map/all_gather | solution.py:44
  55.7 9.9 %copy.19 = bf16[1,4096,192]{2,0,1:T(2,128)(2,1)} copy(bf16[1,4096,192]{1,2,0:T(8,128)(2,1)} %param.4) | data formatting | bytes 3145728 | tf_op args[1]
  66.1 23.6 %reduce = bf16[4096,192]{1,0:T(8,128)(2,1)S(1)} reduce(bf16[4096,1,192]{2,1,0:T(2,128)(2,1)} %bitcast.117, bf16[]{:T(256)} %broadcast.102), dimensions={1}, to_apply=%bitcast.112.reduce_sub_computation | reduce | bytes 3145730
  89.8 4.4 %reshape.54 = bf16[8,2,49152]{2,1,0:T(2,128)(2,1)} reshape(bf16[4096,192]{1,0:T(8,128)(2,1)S(1)} %reduce) | data formatting | bytes 3145728
  94.2 26.3 %all_to_all.4 = bf16[8,2,49152]{2,1,0:T(2,128)(2,1)S(1)} all-to-all(bf16[8,2,49152]{2,1,0:T(2,128)(2,1)} %reshape.54), channel_id=1, replica_groups=mesh['seq'=8,'rep'=16] {'seq'}, dimensions={0} | all-to-all | bytes 3145728 | tf_op jit(solution)/shard_map/all_to_all | solution.py:34
  120.5 4.9 %reshape.55 = bf16[4096,1,192]{2,1,0:T(2,128)(2,1)} reshape(bf16[8,2,49152]{2,1,0:T(2,128)(2,1)S(1)} %all_to_all.4) | data formatting | bytes 3145728
  125.4 10.0 %copy.20 = bf16[1,4096,192]{1,2,0:T(8,128)(2,1)S(1)} copy(bf16[1,4096,192]{2,0,1:T(2,128)(2,1)} %bitcast.118) | data formatting | bytes 3145728 | tf_op jit(solution)/shard_map/all_to_all | solution.py:34
  138.4 3.0 broadcast_in_dim.8
  146.2 3.8 constant_dynamic-update-slice_fusion.1
  152.7 4.8 %collective-permute-start.1 = (bf16[1,2,1536]{2,1,0:T(2,128)(2,1)S(1)}, bf16[1,2,1536]{2,1,0:T(2,128)(2,1)S(1)}, u32[]{:S(2)}, u32[]{:S(2)}) collective-permute-start(bf16[1,2,1536]{2,1,0:T(2,128)(2,1)S(1)} %get-tuple-element.3), channel_id=1, source_target_pairs={{0,16},{16,32},{32,48},{48,64},{64,80},{80,96},{96,112},{1,17},{17... | collective-permute-start | bytes 18440 | tf_op jit(solution)/shard_map/ppermute | solution.py:14
  158.1 6.0 %bitcast_dynamic-update-slice_fusion.4 = f32[5,768,1536]{2,1,0:T(8,128)S(1)} fusion(bf16[1,1026,1536]{2,1,0:T(8,128)(2,1)} %constant_dynamic-update-slice_fusion, bf16[1,1024,768]{2,1,0:T(8,128)(2,1)} %param.3), kind=kOutput, calls=%fused_computation.14 | convolution fusion | flops 2423783424 | bytes 9437184 | tf_op jit(solution)/shard_map/dot_general | solution.py:27
  164.2 3.5 bitcast_dynamic-update-slice_fusion.3
  170.7 13.9 %bitcast_dynamic-update-slice_fusion.1 = f32[5,768,1536]{2,1,0:T(8,128)S(1)} fusion(f32[5,768,1536]{2,1,0:T(8,128)S(1)} %bitcast_dynamic-update-slice_fusion.2, bf16[1,2,1536]{2,1,0:T(2,128)(2,1)S(1)} %collective-permute-done.1, bf16[1,1024,1536]{2,1,0:T(8,128)(2,1)S(1)} %copy-done, bf16[1,1024,768]{2,1,0:T(8,128)(2,1)S(1)} %copy-done.5), kind=kOutput, calls=%fused_computation.11 | convolution fusion | flops 2430074880 | bytes 9443328 | tf_op jit(solution)/shard_map/dot_general | solution.py:27
  184.6 3.5 bitcast_dynamic-update-slice_fusion
  188.1 8.3 %broadcast_multiply_fusion = f32[5,768,1536]{2,1,0:T(8,128)} fusion(f32[5,768,1536]{2,1,0:T(8,128)S(1)} %bitcast_dynamic-update-slice_fusion), kind=kLoop, calls=%fused_computation | loop fusion | flops 5898240 | bytes 47185920 | tf_op jit(solution)/shard_map/mul | solution.py:53
  196.4 7.0 %fusion.24 = f32[1024,768]{1,0:T(8,128)} fusion(bf16[1,1026,1536]{2,1,0:T(8,128)(2,1)} %constant_dynamic-update-slice_fusion, bf16[5,768,1536]{2,1,0:T(8,128)(2,1)} %all-gather.2.cloned.1.call-done), kind=kOutput, calls=%fused_computation.41 | convolution fusion | flops 2415919104 | bytes 8650752 | tf_op jit(solution)/shard_map/dot_general | solution.py:21
  203.4 128.1 %reduce-scatter.5.cloned.1.call-done = f32[5,48,1536]{2,1,0:T(8,128)} async-done(((f32[5,768,1536]{2,1,0:T(8,128)}), f32[5,48,1536]{2,1,0:T(8,128)}) %reduce-scatter.5.cloned.1.call-update) | async-done | bytes 1474576 | tf_op jit(solution)/shard_map/reduce_scatter | solution.py:54
  331.5 5.0 %copy.25 = f32[5,48,1536]{1,0,2:T(8,128)} copy(f32[5,48,1536]{2,1,0:T(8,128)} %reduce-scatter.5.cloned.1.call-done) | data formatting | bytes 2949120
  336.5 4.9 %reshape.52 = f32[1536,240]{1,0:T(8,128)} reshape(f32[1536,5,48]{2,1,0:T(8,128)} %bitcast.116) | data formatting | bytes 2949120
  341.4 4.5 %fusion.26 = f32[1024,768]{1,0:T(8,128)S(1)} fusion(bf16[5,768,1536]{2,1,0:T(8,128)(2,1)} %all-gather.2.cloned.1.call-done, bf16[1,2,1536]{2,1,0:T(2,128)(2,1)S(1)} %collective-permute-done.1, bf16[1,1024,1536]{2,1,0:T(8,128)(2,1)S(1)} %copy-done), kind=kOutput, calls=%fused_computation.45 | convolution fusion | flops 2422210560 | bytes 8656896 | tf_op jit(solution)/shard_map/dot_general | solution.py:21
  345.9 4.4 %fusion.27 = f32[1024,768]{1,0:T(8,128)S(1)} fusion(bf16[1024,1536]{1,0:T(8,128)(2,1)S(1)} %copy-done.2, bf16[5,768,1536]{2,1,0:T(8,128)(2,1)} %all-gather.2.cloned.1.call-done), kind=kOutput, calls=%fused_computation.47 | convolution fusion | flops 2415919104 | bytes 8650752 | tf_op jit(solution)/shard_map/dot_general | solution.py:21
  350.4 4.5 %fusion.23 = f32[1024,768]{1,0:T(8,128)S(1)} fusion(bf16[1,1026,1536]{2,1,0:T(8,128)(2,1)S(1)} %copy-done.4, bf16[5,768,1536]{2,1,0:T(8,128)(2,1)} %all-gather.2.cloned.1.call-done), kind=kOutput, calls=%fused_computation.40 | convolution fusion | flops 2415919104 | bytes 8650752 | tf_op jit(solution)/shard_map/dot_general | solution.py:21
  354.9 7.4 %fusion.31 = bf16[1,1024,768]{2,1,0:T(8,128)(2,1)} fusion(bf16[1,1024,1536]{2,1,0:T(8,128)(2,1)S(1)} %copy-done, bf16[1,1024,768]{2,1,0:T(8,128)(2,1)S(1)} %copy-done.6, f32[1024,768]{1,0:T(8,128)S(1)} %fusion.26, f32[1024,768]{1,0:T(8,128)S(1)} %fusion.27, f32[1024,768]{1,0:T(8,128)S(1)} %fusion.23, f32[1024,768]{1,0:T(8,128)S(1)} %copy-done.7, ...), kind=kOutput, calls=%fused_computation.52 | convolution fusion | flops 2442657792 | bytes 22812672 | tf_op jit(solution)/shard_map/dot_general | solution.py:21
  362.3 52.0 %reduce-scatter.7.cloned.1.call-done = f32[192,240]{1,0:T(8,128)} async-done(((f32[1536,240]{1,0:T(8,128)}), f32[192,240]{1,0:T(8,128)}) %reduce-scatter.7.cloned.1.call-update) | async-done | bytes 184336
  (40 shorter events, 20.6 us)
Async XLA Ops:
  7.2 189.3 %all-gather.2.cloned.1.call-start = ((), (), s32[]{:S(2)}) async-start(), calls=%async_computation.3 | async-start | bytes 12533760 | tf_op jit(solution)/shard_map/all_gather | solution.py:45
  55.6 275.9 %reduce-scatter.5.cloned.1.call-start = ((), (), s32[]{:S(2)}) async-start(), calls=%async_computation.4 | async-start | bytes 25067520 | tf_op jit(solution)/shard_map/reduce_scatter | solution.py:54
  144.9 12.6 %collective-permute-start = (bf16[1,2,1536]{2,1,0:T(2,128)(2,1)S(1)}, bf16[1,2,1536]{2,1,0:T(2,128)(2,1)S(1)}, u32[]{:S(2)}, u32[]{:S(2)}) collective-permute-start(bf16[1,2,1536]{2,1,0:T(2,128)(2,1)S(1)} %get-tuple-element.2), channel_id=1, source_target_pairs={{16,0},{32,16},{48,32},{64,48},{80,64},{96,80},{112,96},{17,1},{33... | collective-permute-start | bytes 18440 | tf_op jit(solution)/shard_map/ppermute | solution.py:15
  152.7 18.0 %collective-permute-start.1 = (bf16[1,2,1536]{2,1,0:T(2,128)(2,1)S(1)}, bf16[1,2,1536]{2,1,0:T(2,128)(2,1)S(1)}, u32[]{:S(2)}, u32[]{:S(2)}) collective-permute-start(bf16[1,2,1536]{2,1,0:T(2,128)(2,1)S(1)} %get-tuple-element.3), channel_id=1, source_target_pairs={{0,16},{16,32},{32,48},{48,64},{64,80},{80,96},{96,112},{1,17},{17... | collective-permute-start | bytes 18440 | tf_op jit(solution)/shard_map/ppermute | solution.py:14
  158.1 6.0 %copy-start.3 = (bf16[1,1026,1536]{2,1,0:T(8,128)(2,1)S(1)}, bf16[1,1026,1536]{2,1,0:T(8,128)(2,1)}, u32[]{:S(2)}) copy-start(bf16[1,1026,1536]{2,1,0:T(8,128)(2,1)} %constant_dynamic-update-slice_fusion) | copy-start | bytes 9455620
  158.1 6.0 %copy-start.5 = (bf16[1,1024,768]{2,1,0:T(8,128)(2,1)S(1)}, bf16[1,1024,768]{2,1,0:T(8,128)(2,1)}, u32[]{:S(2)}) copy-start(bf16[1,1024,768]{2,1,0:T(8,128)(2,1)} %param.3) | copy-start | bytes 4718596
  164.1 3.5 copy-start.1
  167.7 3.0 copy-start
  196.4 217.9 %reduce-scatter.7.cloned.1.call-start = ((), (), s32[]{:S(2)}) async-start(), calls=%async_computation.5 | async-start | bytes 1769472
  341.4 4.5 %copy-start.2 = (bf16[1024,1536]{1,0:T(8,128)(2,1)S(1)}, bf16[1024,1536]{1,0:T(8,128)(2,1)}, u32[]{:S(2)}) copy-start(bf16[1024,1536]{1,0:T(8,128)(2,1)} %broadcast_in_dim.9) | copy-start | bytes 9437188
  345.9 4.5 %copy-start.4 = (bf16[1,1026,1536]{2,1,0:T(8,128)(2,1)S(1)}, bf16[1,1026,1536]{2,1,0:T(8,128)(2,1)}, u32[]{:S(2)}) copy-start(bf16[1,1026,1536]{2,1,0:T(8,128)(2,1)} %constant_dynamic-update-slice_fusion) | copy-start | bytes 9455620
  350.4 4.5 %copy-start.6 = (bf16[1,1024,768]{2,1,0:T(8,128)(2,1)S(1)}, bf16[1,1024,768]{2,1,0:T(8,128)(2,1)}, u32[]{:S(2)}) copy-start(bf16[1,1024,768]{2,1,0:T(8,128)(2,1)} %param.3) | copy-start | bytes 4718596
  350.4 4.5 %copy-start.7 = (f32[1024,768]{1,0:T(8,128)S(1)}, f32[1024,768]{1,0:T(8,128)}, u32[]{:S(2)}) copy-start(f32[1024,768]{1,0:T(8,128)} %fusion.24) | copy-start | bytes 9437188
Sparse Core Ops, SparseCore 0:
  55.8 84.3 all-gather.1
  196.5 134.9 reduce-scatter.4
  341.5 72.7 reduce-scatter.6
where the time goes:
time: 426 us; the launch traced here: 423 us
  waiting for transfers between devices  180 us (42%)
  blocking collectives  71 us (17%)
  local copies, waits for them, and re-layouts  61.7 us (14%)
  matrix products  57.5 us (13%)
  other arithmetic  32.2 us (8%)
  between operations  14.2 us (3%)
  starting transfers between devices  6.2 us (1%)
    reduce_scatter x1, waiting for transfers between devices, on_device(): lax.psum_scatter(terms, 'rep', scatter_dimension=1, tiled=True)  128 us
    unnamed x4, waiting for transfers between devices  52.1 us
    all_gather x1, blocking collectives, on_device(): columns = lax.all_gather(weights, 'seq', axis=2, tiled=True)  44.7 us
    unnamed x27, local copies, waits for them, and re-layouts  37.3 us
    dot_general x5, matrix products, contract_first(): lax.dot_general(left, right, (((0,), (0,)), ((), ())), preferred_element_...  29.8 us
    dot_general x5, matrix products, contract_last(): lax.dot_general(left, right, (((1,), (1,)), ((), ())), preferred_element_...  27.7 us
    all_to_all x1, blocking collectives, on_device(): lax.all_to_all(trunk_grad, 'seq', split_axis=1, concat_axis=2, tiled=True)  26.3 us
    unnamed x1, other arithmetic  23.6 us
  transfers between devices with their start and end apart: 5, of which 2 were waited for; matrix products, arithmetic and copies ran while one was open for 32% of the time, Pallas kernels for 0%

commit v1 on v0

v1 whole, which is shorter than its diff:
```python
import functools

import jax
import jax.numpy as jnp
from jax import lax
from jax.experimental import pallas as pl
from jax.experimental.pallas import tpu as pltpu
from jax.sharding import PartitionSpec as P

MESH = pl.DeviceIdType.MESH
BF = jnp.bfloat16
F32 = jnp.float32

CIN, COUT, KW = 768, 1536, 5
HALF = CIN // 2
ROWS = 512
HALO = 16
EXT = ROWS + 2 * HALO
BLK = 48
PIECE = 368
PARTS = ((0, 128), (128, 128), (256, 112))


def nt(left, right):
    return lax.dot_general(
        left, right, (((1,), (1,)), ((), ())), preferred_element_type=F32
    )


def nn(left, right):
    return jnp.dot(left, right, preferred_element_type=F32)


def low_lanes(shape):
    return lax.broadcasted_iota(jnp.int32, shape, len(shape) - 1) < 64


def swap(value):
    return pltpu.roll(value, 64, 1)


def pack(direct, other):
    low = low_lanes(direct.shape)
    rolled = swap(other)
    return jnp.where(low, direct, rolled), jnp.where(low, rolled, direct)


def unpack(first, second):
    low = low_lanes(first.shape)
    return jnp.where(low, first, second), swap(jnp.where(low, second, first))


def channel_of(column, core):
    other = column >= HALF
    col = jnp.where(other, column - HALF, column)
    block = jnp.zeros_like(col)
    for t in range(1, 8):
        block = block + (col >= t * BLK).astype(jnp.int32)
    parity = jnp.where(other, 1 - core, core)
    return (2 * block + parity) * BLK + (col - block * BLK)


def kernel(
    x_hbm, g_hbm, w_hbm, dx_ref, wg_ref,
    xin, gin, win, smain, stail, gbuf, tails, gs, shifty, perm, sel,
    xh, xo, xr, xr2, do, eot, slope, wa, wfull, wg, r1a, r1b, r1c,
    s1a, s1b, s1c, r2a, r2b, r2c, s2a, s2b, s2c, r3a, r3b, r3c, fin, p1, p3,
    lsem, ssem, rsem,
):
    s = lax.axis_index("seq")
    r = lax.axis_index("rep")
    x, yhi = lax.rem(s, 4), s // 4
    ylo, z, core = r // 8, lax.rem(r // 2, 4), lax.rem(r, 2)
    y = yhi * 2 + ylo
    odd = lax.rem(x, 2) == 1

    def dev(px, py, pz, pc):
        return ((py // 2) * 4 + px, (lax.rem(py, 2) * 4 + pz) * 2 + pc)

    def at(axis, d):
        c = {"x": x, "y": y, "z": z}
        c[axis] = lax.rem(c[axis] + d, 4)
        return dev(c["x"], c["y"], c["z"], core), c[axis]

    other_core = dev(x, y, z, 1 - core)

    load_x = pltpu.make_async_copy(x_hbm.at[0], xin, lsem.at[0])
    load_g = pltpu.make_async_copy(g_hbm.at[0], gin, lsem.at[1])
    load_w = pltpu.make_async_copy(w_hbm, win, lsem.at[2])
    load_w.start()
    load_g.start()
    load_x.start()

    barrier = pltpu.get_barrier_semaphore()
    friends = [at(axis, d)[0] for axis in "xyz" for d in (1, 2, 3)]
    friends += [dev(lax.rem(x + d, 4), lax.rem(y + 2, 4), z, core) for d in (1, 2, 3)]
    friends.append(other_core)
    for friend in friends:
        pl.semaphore_signal(barrier, inc=1, device_id=friend, device_id_type=MESH)

    count = [0]

    def remote(src, dst, device):
        i = count[0]
        count[0] += 1
        return pltpu.make_async_remote_copy(
            src_ref=src, dst_ref=dst, send_sem=ssem.at[i], recv_sem=rsem.at[i],
            device_id=device, device_id_type=MESH,
        )

    load_w.wait()
    mine = wa.at[x, y, z]

    def tail_of(tap):
        return win[tap, :, 128:192].astype(F32)

    def placed(first, second):
        both = jnp.concatenate([first, second], axis=1)
        return jnp.where(odd, swap(both), both).astype(BF)

    for tap in range(KW):
        mine[tap * BLK : (tap + 1) * BLK, :] = win[tap, :, :128]
    mine[240:288, :] = placed(tail_of(0), tail_of(1))
    mine[288:336, :] = placed(tail_of(2), tail_of(3))
    last = tail_of(4)
    mine[336:368, :] = placed(
        last[:32], jnp.concatenate([last[32:], jnp.zeros((16, 64), F32)], axis=0)
    )

    pl.semaphore_wait(barrier, len(friends))

    ranges = [pl.ds(start, size) for start, size in PARTS]
    ga, gb, gc = ranges

    def spread(axis, ref):
        copies = [remote(ref, ref, at(axis, d)[0]) for d in (1, 2, 3)]
        for c in copies:
            c.start()
        return copies

    gather1 = (
        spread("x", wa.at[x, y, z, ga])
        + spread("y", wa.at[x, y, z, gb])
        + spread("z", wa.at[x, y, z, gc])
    )

    load_g.wait()
    smain[0:HALO, :] = jnp.zeros((HALO, 128), BF)
    smain[HALO + 4096 : 2 * HALO + 4096, :] = jnp.zeros((HALO, 128), BF)

    @pl.loop(0, 8)
    def _(part):
        rows = pl.ds(pl.multiple_of(part * 512, 512), 512)
        smain[pl.ds(pl.multiple_of(part * 512 + HALO, 16), 512), :] = gin[rows, :128]

    def tail_rows(start):
        return gin[pl.ds(pl.multiple_of(start, 16), 256), 128:192].astype(F32)

    @pl.loop(0, 8)
    def _(part):
        base = part * 512
        before = gin[
            pl.ds(pl.multiple_of(jnp.maximum(base - HALO, 0), 16), HALO), 128:192
        ].astype(F32)
        before = jnp.where(part == 0, 0.0, before)
        after = gin[
            pl.ds(pl.multiple_of(jnp.minimum(base + 512, 4096 - HALO), 16), HALO), 128:192
        ].astype(F32)
        after = jnp.where(part == 7, 0.0, after)
        top = jnp.concatenate([before, tail_rows(base)], axis=0)
        bottom = jnp.concatenate([tail_rows(base + 256), after], axis=0)
        stail[part] = placed(top, bottom)

    scatter_g = []
    for dy in (0, 1):
        for dx_ in range(4):
            if dx_ == 0 and dy == 0:
                continue
            px, phi = lax.rem(x + dx_, 4), lax.rem(yhi + dy, 2)
            ps = phi * 4 + px
            target = dev(px, phi * 2 + ylo, z, core)
            rows = pl.ds(pl.multiple_of(ps * 512, 512), EXT)
            scatter_g.append(remote(smain.at[rows], gbuf.at[0, s], target))
            scatter_g.append(remote(stail.at[ps], tails.at[s], target))
    for c in scatter_g:
        c.start()
    gbuf[0, s] = smain[pl.ds(pl.multiple_of(s * 512, 512), EXT), :]
    tails[s] = stail[s]

    row_i = lax.broadcasted_iota(jnp.int32, (CIN, CIN), 0)
    col_i = lax.broadcasted_iota(jnp.int32, (CIN, CIN), 1)
    perm[...] = jnp.where(row_i == channel_of(col_i, core), 1.0, 0.0).astype(BF)

    load_x.wait()

    @pl.loop(0, 4)
    def _(part):
        rows = pl.ds(pl.multiple_of(part * 256, 256), 256)
        ordered = nn(xin[rows, :], perm[...])
        for c in range(3):
            xh[0, c, rows, :] = ordered[:, c * 128 : (c + 1) * 128]
        xo[rows, :] = ordered[:, HALF:].astype(BF)

    swap_x = remote(xo, xr, other_core)
    swap_x.start()

    for c in gather1:
        c.wait()
    gather2 = (
        spread("y", wa.at[:, y, z, ga])
        + spread("z", wa.at[x, :, z, gb])
        + spread("x", wa.at[x, y, :, gc])
    )

    def activate(q, part):
        for phase in (0, 1):
            for c in range(3):
                v = xh[q, c, pl.ds(part * 256 + phase, 128, stride=2), :]
                sq = v * v
                u = 0.7978845608028654 * (v + 0.044715 * (sq * v))
                t = jnp.tanh(u)
                half = 0.5 * (1.0 + t)
                act = (v * half).astype(BF)
                grad = half + 0.5 * v * (1.0 - t * t) * (
                    0.7978845608028654 * (1.0 + 3.0 * 0.044715 * sq)
                )
                cols = pl.ds(pl.multiple_of(q * 512 + part * 128, 128), 128)
                lo = phase * HALF + c * 128
                eot[lo : lo + 128, cols] = act.astype(F32).T.astype(BF)
                slope[phase, c, cols, :] = grad

    @pl.loop(0, 4)
    def _(part):
        activate(0, part)

    for c in gather2:
        c.wait()
    gather3 = (
        spread("z", wa.at[:, :, z, ga])
        + spread("x", wa.at[x, :, :, gb])
        + spread("y", wa.at[:, y, :, gc])
    )

    swap_x.wait()

    @pl.loop(0, 4)
    def _(part):
        rows = pl.ds(pl.multiple_of(part * 256, 256), 256)
        for c in range(3):
            xh[1, c, rows, :] = xr[rows, c * 128 : (c + 1) * 128].astype(F32)

    @pl.loop(0, 4)
    def _(part):
        activate(1, part)

    row_s = lax.broadcasted_iota(jnp.int32, (CIN, HALF), 0)
    col_s = lax.broadcasted_iota(jnp.int32, (CIN, HALF), 1)
    is_tail = row_s >= 512
    tail_s = (row_s - 512) // 64
    natural = jnp.where(
        is_tail,
        tail_s * 192 + 128 + (row_s - 512 - tail_s * 64),
        (row_s // 128) * 192 + lax.rem(row_s, 128),
    )
    sel[...] = jnp.where(natural == channel_of(col_s, core), 1.0, 0.0).astype(BF)

    for c in scatter_g:
        c.wait()

    @pl.loop(0, 4)
    def _(m):
        top, bottom = unpack(tails[2 * m].astype(F32), tails[2 * m + 1].astype(F32))
        gbuf[0, 8 + m, 0 : EXT // 2, :] = top.astype(BF)
        gbuf[0, 8 + m, EXT // 2 : EXT, :] = bottom.astype(BF)

    swap_g = remote(gbuf.at[0], gbuf.at[1], other_core)
    swap_g.start()

    def shifted(q):
        rows = slice(q * ROWS, (q + 1) * ROWS)

        @pl.loop(0, 12)
        def _(t):
            cols = pl.ds(pl.multiple_of(t * 128, 128), 128)
            shifty[...] = gbuf[q, t].astype(F32)
            for j in (0, 1, 2):
                gs[j, rows, cols] = shifty[HALO - 1 + j : HALO - 1 + j + ROWS, :].astype(BF)

    shifted(0)
    swap_g.wait()
    shifted(1)

    scale = 0.5 * float(16 * 8192) ** (-0.5)

    def grads(start):
        cols = pl.ds(pl.multiple_of(start, 128), 256)
        sums = [nn(eot[...], gs[j, :, cols]) * scale for j in (0, 1, 2)]
        a = [v[:HALF] for v in sums]
        b = [v[HALF:] for v in sums]
        return (a[2] + b[2], a[1] + b[2], a[1] + b[1], a[0] + b[1], a[0] + b[0])

    @pl.loop(0, 4)
    def _(n):
        taps = grads(n * 256)
        for half in (0, 1):
            px = lax.rem(n, 2) * 2 + half
            for b in range(8):
                target = wg.at[px, (n // 2) * 2 + b // 4, b % 4]
                for k in range(KW):
                    target[k * BLK : (k + 1) * BLK, :] = taps[k][
                        b * BLK : (b + 1) * BLK, half * 128 : (half + 1) * 128
                    ].astype(BF)

    @pl.loop(0, 2)
    def _(n):
        taps = grads(1024 + n * 256)
        for m in (0, 1):
            lanes = slice(m * 128, (m + 1) * 128)
            for b in range(8):
                rows = slice(b * BLK, (b + 1) * BLK)
                v = [tap[rows, lanes] for tap in taps]
                first = wg.at[m * 2, n * 2 + b // 4, b % 4]
                second = wg.at[m * 2 + 1, n * 2 + b // 4, b % 4]
                for lo, hi, one, two in (
                    (240, 288, v[0], v[1]),
                    (288, 336, v[2], v[3]),
                    (
                        336, 368, v[4][:32],
                        jnp.concatenate([v[4][32:], jnp.zeros((16, 128), F32)], axis=0),
                    ),
                ):
                    left, right = pack(one, two)
                    first[lo:hi, :] = left.astype(BF)
                    second[lo:hi, :] = right.astype(BF)

    def send_sums(axis, source, slots):
        copies = []
        for d in (1, 2, 3):
            device, c = at(axis, d)
            copies.append(remote(source(c), slots.at[d - 1], device))
        for c in copies:
            c.start()
        return copies

    reduce1 = (
        send_sums("z", lambda c: wg.at[:, :, c, ga], r1a)
        + send_sums("x", lambda c: wg.at[c, :, :, gb], r1b)
        + send_sums("y", lambda c: wg.at[:, c, :, gc], r1c)
    )

    for c in gather3:
        c.wait()

    @pl.loop(0, 8)
    def _(b):
        bhi, blo = b // 4, lax.rem(b, 4)
        base = b * BLK
        rows = pl.ds(pl.multiple_of(base, 16), BLK)
        for t in range(8):
            source = wa.at[t % 4, (t // 4) * 2 + bhi, blo]
            for k in range(KW):
                wfull[k, rows, t * 128 : (t + 1) * 128] = source[k * BLK : (k + 1) * BLK, :]
        for m in range(4):
            lanes = slice(1024 + m * 128, 1152 + m * 128)
            first = wa.at[(2 * m) % 4, (m // 2) * 2 + bhi, blo]
            second = wa.at[(2 * m + 1) % 4, (m // 2) * 2 + bhi, blo]
            for lo, k in ((240, 0), (288, 2)):
                one, two = unpack(
                    first[lo : lo + BLK, :].astype(F32), second[lo : lo + BLK, :].astype(F32)
                )
                wfull[k, rows, lanes] = one.astype(BF)
                wfull[k + 1, rows, lanes] = two.astype(BF)
            one, two = unpack(first[336:368, :].astype(F32), second[336:368, :].astype(F32))
            wfull[4, pl.ds(pl.multiple_of(base, 16), 32), lanes] = one.astype(BF)
            wfull[4, pl.ds(pl.multiple_of(base + 32, 16), 16), lanes] = two[:16].astype(BF)

    def inputs_back(q):
        @pl.loop(0, 2)
        def _(part):
            rows = pl.ds(pl.multiple_of(q * 512 + part * 256, 256), 256)
            middle = gs[1, rows, :]
            shared = (
                nt(gs[2, rows, :], wfull[0])
                + nt(middle, wfull[2])
                + nt(gs[0, rows, :], wfull[4])
            )
            p1[...] = nt(gs[1, rows, :], wfull[1])
            p3[...] = nt(gs[1, rows, :], wfull[3])
            after = nt(gs[2, rows, :], wfull[1])
            before = nt(gs[0, rows, :], wfull[3])
            skip = nn(
                jnp.concatenate([middle[:, :512], middle[:, 1024:1280]], axis=1), sel[...]
            )
            even = shared + p1[...] + before
            odd_ = shared + after + p3[...]
            for phase, value in ((0, even), (1, odd_)):
                for c in range(3):
                    lanes = slice(c * 128, (c + 1) * 128)
                    out = 0.5 * (value[:, lanes] * slope[phase, c, rows, :] + skip[:, lanes])
                    xh[q, c, pl.ds(part * 512 + phase, 256, stride=2), :] = out

    inputs_back(1)

    @pl.loop(0, 4)
    def _(part):
        rows = pl.ds(pl.multiple_of(part * 256, 256), 256)
        for c in range(3):
            do[rows, c * 128 : (c + 1) * 128] = xh[1, c, rows, :].astype(BF)

    swap_d = remote(do, xr2, other_core)
    swap_d.start()
    inputs_back(0)

    for c in reduce1:
        c.wait()

    def add_up(own, slots, out, lead):
        @pl.loop(0, lead[0])
        def _(i):
            for j in range(lead[1]):
                total = own(i, j).astype(F32)
                for d in range(3):
                    total = total + slots[d, i, j].astype(F32)
                out[i, j] = total.astype(out.dtype)

    add_up(lambda i, j: wg[i, j, z, ga, :], r1a, s1a, (4, 4))
    add_up(lambda i, j: wg[x, i, j, gb, :], r1b, s1b, (4, 4))
    add_up(lambda i, j: wg[i, y, j, gc, :], r1c, s1c, (4, 4))
    reduce2 = (
        send_sums("y", lambda c: s1a.at[:, c], r2a)
        + send_sums("z", lambda c: s1b.at[:, c], r2b)
        + send_sums("x", lambda c: s1c.at[c], r2c)
    )

    swap_d.wait()

    @pl.loop(0, 4)
    def _(part):
        rows = pl.ds(pl.multiple_of(part * 256, 256), 256)
        both = jnp.concatenate(
            [xh[0, c, rows, :].astype(BF) for c in range(3)] + [xr2[rows, :]], axis=1
        )
        dx_ref[0, rows, :] = nt(both, perm[...]).astype(BF)

    for c in reduce2:
        c.wait()

    def add_up2(own, slots, out):
        for i in range(4):
            total = own(i).astype(F32)
            for d in range(3):
                total = total + slots[d, i].astype(F32)
            out[i] = total

    add_up2(lambda i: s1a[i, y], r2a, s2a)
    add_up2(lambda i: s1b[i, z], r2b, s2b)
    add_up2(lambda i: s1c[x, i], r2c, s2c)
    reduce3 = (
        send_sums("x", lambda c: s2a.at[c], r3a)
        + send_sums("y", lambda c: s2b.at[c], r3b)
        + send_sums("z", lambda c: s2c.at[c], r3c)
    )
    for c in reduce3:
        c.wait()
    for (start, size), own, slots in zip(
        PARTS, (s2a[x], s2b[y], s2c[z]), (r3a, r3b, r3c)
    ):
        fin[start : start + size, :] = own + slots[0] + slots[1] + slots[2]
    for k in range(KW):
        wg_ref[k, :, 0:128] = fin[k * BLK : (k + 1) * BLK, :]

    def unplaced(lo, hi):
        value = fin[lo:hi, :]
        value = jnp.where(odd, swap(value), value)
        return value[:, :64], swap(value)[:, :64]

    for lo, k in ((240, 0), (288, 2)):
        one, two = unplaced(lo, lo + BLK)
        wg_ref[k, :, 128:192] = one
        wg_ref[k + 1, :, 128:192] = two
    one, two = unplaced(336, 368)
    wg_ref[4, 0:32, 128:192] = one
    wg_ref[4, 32:48, 128:192] = two[:16]


def on_device(inputs, trunk_grad, weights):
    sizes = [size for _, size in PARTS]
    vm = pltpu.VMEM
    scratch = [
        vm((1024, CIN), BF), vm((4096, 192), BF), vm((KW, BLK, 192), BF),
        vm((4096 + 2 * HALO, 128), BF), vm((8, EXT // 2, 128), BF),
        vm((2, 12, EXT, 128), BF), vm((8, EXT // 2, 128), BF),
        vm((3, 2 * ROWS, COUT), BF), vm((EXT, 128), F32),
        vm((CIN, CIN), BF), vm((CIN, HALF), BF),
        vm((2, 3, 1024, 128), F32), vm((1024, HALF), BF), vm((1024, HALF), BF),
        vm((1024, HALF), BF), vm((1024, HALF), BF),
        vm((CIN, 1024), BF), vm((2, 3, 1024, 128), F32),
        vm((4, 4, 4, PIECE, 128), BF), vm((KW, HALF, COUT), BF),
        vm((4, 4, 4, PIECE, 128), BF),
    ]
    scratch += [vm((3, 4, 4, n, 128), BF) for n in sizes]
    scratch += [vm((4, 4, n, 128), BF) for n in sizes]
    scratch += [vm((3, 4, n, 128), BF) for n in sizes]
    scratch += [vm((4, n, 128), F32) for n in sizes]
    scratch += [vm((3, n, 128), F32) for n in sizes]
    scratch += [vm((PIECE, 128), F32), vm((256, HALF), F32), vm((256, HALF), F32)]
    copies = 27 + 14 + 3 + 27
    scratch += [
        pltpu.SemaphoreType.DMA((3,)),
        pltpu.SemaphoreType.DMA((copies,)),
        pltpu.SemaphoreType.DMA((copies,)),
    ]
    return pl.pallas_call(
        kernel,
        out_shape=(
            jax.ShapeDtypeStruct((1, 1024, CIN), BF),
            jax.ShapeDtypeStruct((KW, BLK, 192), F32),
        ),
        in_specs=[pl.BlockSpec(memory_space=pl.ANY)] * 3,
        out_specs=(pl.BlockSpec(memory_space=pltpu.VMEM),) * 2,
        scratch_shapes=scratch,
        compiler_params=pltpu.CompilerParams(
            collective_id=0, has_side_effects=True, vmem_limit_bytes=63 * 1024 * 1024
        ),
        name="block_backward",
    )(inputs, trunk_grad, weights)


def solution(mesh):
    in_specs = (P("rep", "seq", None), P("rep", None, "seq"), P(None, "rep", "seq"))
    out_specs = (P("rep", "seq", None), P(None, "rep", "seq"))
    return jax.shard_map(
        on_device, mesh=mesh, in_specs=in_specs, out_specs=out_specs, check_vma=False
    )
```

time: 426 us -> 111 us (0.26)
  waiting for transfers between devices: 180 us -> 0 us
  Pallas kernels: 0 us -> 103 us
  blocking collectives: 71 us -> 0 us
  matrix products: 57.5 us -> 0 us
  local copies, waits for them, and re-layouts: 61.7 us -> 7.25 us
  other arithmetic: 32.2 us -> 0 us
  between operations: 14.2 us -> 0.65 us
  starting transfers between devices: 6.2 us -> 0 us
    reduce_scatter x1 -> x0, waiting for transfers between devices: 128 us -> none  [on_device(): lax.psum_scatter(terms, 'rep', scatter_dimension=1, tiled=True)]
    pallas_call x0 -> x1, Pallas kernels: none -> 103 us  [on_device(): pl.pallas_call(kernel, out_shape=(jax.ShapeDtypeStruct((1, 1024, CIN), BF...]
    dot_general x10 -> x0, matrix products: 57.5 us -> none  [the longest x5 29.8 us: contract_first(): lax.dot_general(left, right, (((0,), (0,)), ((), ())), preferred_element_...]
    unnamed x4 -> x0, waiting for transfers between devices: 52.1 us -> none
    all_gather x1 -> x0, blocking collectives: 44.7 us -> none  [on_device(): columns = lax.all_gather(weights, 'seq', axis=2, tiled=True)]
    unnamed x27 -> x5, local copies, waits for them, and re-layouts: 37.3 us -> 7.25 us
    all_to_all x1 -> x0, blocking collectives: 26.3 us -> none  [on_device(): lax.all_to_all(trunk_grad, 'seq', split_axis=1, concat_axis=2, tiled=True)]
    unnamed x1 -> x0, other arithmetic: 23.6 us -> none
  transfers between devices with their start and end apart: 5 -> 0, of which waited for: 2 -> 0; matrix products, arithmetic and copies ran while one was open for 32% -> 0% of each run, Pallas kernels for 0% -> 0%
where the time goes in v1:
time: 111 us
  Pallas kernels  103 us (93%)
  local copies, waits for them, and re-layouts  7.25 us (7%)
    pallas_call x1, Pallas kernels, on_device(): pl.pallas_call(kernel, out_shape=(jax.ShapeDtypeStruct((1, 1024, CIN), BF...  103 us
    unnamed x5, local copies, waits for them, and re-layouts  7.25 us

profile of v1, /device:TPU:0, one launch (start us, length us, event | category | flops | bytes accessed | tf_op | source)
XLA Modules:
  0.0 111.0 jit_solution(9416261467805292117)
XLA Ops:
  0.6 3.9 %copy.5.g_hbm = bf16[1,4096,192]{2,1,0:T(8,128)(2,1)} copy(bf16[1,4096,192]{1,2,0:T(8,128)(2,1)} %param.4) | data formatting | bytes 3145728 | tf_op args[1]
  4.5 103.1 %block_backward.1 = (bf16[1,1024,768]{2,1,0:T(8,128)(2,1)}, f32[5,48,192]{2,1,0:T(8,128)}) custom-call(bf16[1,1024,768]{2,1,0:T(8,128)(2,1)} %x_hbm.1, bf16[1,4096,192]{2,1,0:T(8,128)(2,1)} %copy.5.g_hbm, bf16[5,48,192]{2,1,0:T(8,128)(2,1)} %w_hbm.1), custom_call_target="tpu_custom_call" | custom-call | tf_op jit(solution)/shard_map/block_backward/pallas_call | solution.py:513
  107.6 0.0 copy-start
  107.6 2.7 %copy.8 = bf16[1,1024,768]{2,1,0:T(8,128)(2,1)} copy(bf16[1,1024,768]{2,1,0:T(8,128)(2,1)} %get-tuple-element.4) | data formatting | bytes 3145728
  110.3 0.0 copy-done
  110.3 0.7 copy.9
Async XLA Ops:
  107.6 2.7 %copy-start = (f32[5,48,192]{2,1,0:T(8,128)S(1)}, f32[5,48,192]{2,1,0:T(8,128)}, u32[]{:S(2)}) copy-start(f32[5,48,192]{2,1,0:T(8,128)} %get-tuple-element.5) | copy-start | bytes 552964

commit v2 on v1

--- a/solution.py
+++ b/solution.py
@@ -18,7 +18,9 @@
 EXT = ROWS + 2 * HALO
 BLK = 48
 PIECE = 368
-PARTS = ((0, 128), (128, 128), (256, 112))
+GATHER = ((0, 128), (128, 128), (256, 112))
+REDUCE = (((0, 80), (80, 80), (160, 80)), ((240, 48), (288, 48), (336, 32)))
+TILE = 288
 
 
 def nt(left, right):
@@ -62,11 +64,14 @@
 
 def kernel(
     x_hbm, g_hbm, w_hbm, dx_ref, wg_ref,
-    xin, gin, win, smain, stail, gbuf, tails, gs, shifty, perm, sel,
-    xh, xo, xr, xr2, do, eot, slope, wa, wfull, wg, r1a, r1b, r1c,
-    s1a, s1b, s1c, r2a, r2b, r2c, s2a, s2b, s2c, r3a, r3b, r3c, fin, p1, p3,
-    lsem, ssem, rsem,
+    xin, gin, win, gpad, stail, grad, tails, perm, sel,
+    xh, xo, xr, xr2, do, et, eot, slope, wa, wfull, wg, prod, fin, *rest,
 ):
+    def four(n):
+        return [[rest[n * 6 + g * 3 + p] for p in range(3)] for g in range(2)]
+
+    r1, s1, r2, s2, r3 = [four(n) for n in range(5)]
+    lsem, ssem, rsem = rest[30:]
     s = lax.axis_index("seq")
     r = lax.axis_index("rep")
     x, yhi = lax.rem(s, 4), s // 4
@@ -127,49 +132,85 @@
         last[:32], jnp.concatenate([last[32:], jnp.zeros((16, 64), F32)], axis=0)
     )
 
-    pl.semaphore_wait(barrier, len(friends))
-
-    ranges = [pl.ds(start, size) for start, size in PARTS]
-    ga, gb, gc = ranges
-
-    def spread(axis, ref):
-        copies = [remote(ref, ref, at(axis, d)[0]) for d in (1, 2, 3)]
+    ga, gb, gc = [pl.ds(start, size) for start, size in GATHER]
+    ahead = 1 - 2 * core
+
+    def at_ahead(axis, n):
+        return at(axis, n * ahead + 4)
+
+    class Line:
+        def __init__(self, axis, block):
+            self.axis, self.block = axis, block
+            self.onward, _ = at_ahead(axis, 1)
+            back, self.before = at_ahead(axis, -1)
+            own = block({"x": x, "y": y, "z": z}[axis])
+            self.first = remote(own, own, self.onward)
+            self.second = remote(own, own, back)
+            self.first.start()
+            self.second.start()
+
+        def relay(self):
+            self.first.wait_recv()
+            block = self.block(self.before)
+            self.third = remote(block, block, self.onward)
+            self.third.start()
+
+        def finish(self):
+            self.first.wait_send()
+            self.second.wait()
+            self.third.wait()
+
+    def relay(lines):
+        for line in lines:
+            line.relay()
+
+    def finish(lines):
+        for line in lines:
+            line.finish()
+
+    def spread(axis, block):
+        copies = [remote(block, block, at(axis, d)[0]) for d in (1, 2, 3)]
         for c in copies:
             c.start()
         return copies
+
+    def settle(copies):
+        for c in copies:
+            c.wait()
+
+    load_g.wait()
+    gpad[0:HALO, :] = jnp.zeros((HALO, 192), BF)
+    gpad[HALO + 4096 : 2 * HALO + 4096, :] = jnp.zeros((HALO, 192), BF)
+
+    @pl.loop(0, 8)
+    def _(part):
+        cols = pl.ds(pl.multiple_of(part * 512, 512), 512)
+        gpad[pl.ds(pl.multiple_of(part * 512 + HALO, 16), 512), :] = gin[:, cols].T
+
+    @pl.loop(0, 8)
+    def _(part):
+        def half(start):
+            rows = pl.ds(pl.multiple_of(part * 512 + start, 16), EXT // 2)
+            return gpad[rows, 128:192].astype(F32)
+
+        stail[part] = placed(half(0), half(EXT // 2))
+
+    my_lanes = pl.ds(pl.multiple_of(s * 128, 128), 128)
+    grad[0, :, my_lanes] = gpad[pl.ds(pl.multiple_of(s * 512, 512), EXT), 0:128]
+    tails[s] = stail[s]
+
+    row_i = lax.broadcasted_iota(jnp.int32, (CIN, CIN), 0)
+    col_i = lax.broadcasted_iota(jnp.int32, (CIN, CIN), 1)
+    perm[...] = jnp.where(row_i == channel_of(col_i, core), 1.0, 0.0).astype(BF)
+
+    pl.semaphore_wait(barrier, len(friends))
+
 
     gather1 = (
         spread("x", wa.at[x, y, z, ga])
         + spread("y", wa.at[x, y, z, gb])
         + spread("z", wa.at[x, y, z, gc])
     )
-
-    load_g.wait()
-    smain[0:HALO, :] = jnp.zeros((HALO, 128), BF)
-    smain[HALO + 4096 : 2 * HALO + 4096, :] = jnp.zeros((HALO, 128), BF)
-
-    @pl.loop(0, 8)
-    def _(part):
-        rows = pl.ds(pl.multiple_of(part * 512, 512), 512)
-        smain[pl.ds(pl.multiple_of(part * 512 + HALO, 16), 512), :] = gin[rows, :128]
-
-    def tail_rows(start):
-        return gin[pl.ds(pl.multiple_of(start, 16), 256), 128:192].astype(F32)
-
-    @pl.loop(0, 8)
-    def _(part):
-        base = part * 512
-        before = gin[
-            pl.ds(pl.multiple_of(jnp.maximum(base - HALO, 0), 16), HALO), 128:192
-        ].astype(F32)
-        before = jnp.where(part == 0, 0.0, before)
-        after = gin[
-            pl.ds(pl.multiple_of(jnp.minimum(base + 512, 4096 - HALO), 16), HALO), 128:192
-        ].astype(F32)
-        after = jnp.where(part == 7, 0.0, after)
-        top = jnp.concatenate([before, tail_rows(base)], axis=0)
-        bottom = jnp.concatenate([tail_rows(base + 256), after], axis=0)
-        stail[part] = placed(top, bottom)
 
     scatter_g = []
     for dy in (0, 1):
@@ -180,16 +221,10 @@
             ps = phi * 4 + px
             target = dev(px, phi * 2 + ylo, z, core)
             rows = pl.ds(pl.multiple_of(ps * 512, 512), EXT)
-            scatter_g.append(remote(smain.at[rows], gbuf.at[0, s], target))
+            scatter_g.append(remote(gpad.at[rows, 0:128], grad.at[0, :, my_lanes], target))
             scatter_g.append(remote(stail.at[ps], tails.at[s], target))
     for c in scatter_g:
         c.start()
-    gbuf[0, s] = smain[pl.ds(pl.multiple_of(s * 512, 512), EXT), :]
-    tails[s] = stail[s]
-
-    row_i = lax.broadcasted_iota(jnp.int32, (CIN, CIN), 0)
-    col_i = lax.broadcasted_iota(jnp.int32, (CIN, CIN), 1)
-    perm[...] = jnp.where(row_i == channel_of(col_i, core), 1.0, 0.0).astype(BF)
 
     load_x.wait()
 
@@ -204,8 +239,7 @@
     swap_x = remote(xo, xr, other_core)
     swap_x.start()
 
-    for c in gather1:
-        c.wait()
+    settle(gather1)
     gather2 = (
         spread("y", wa.at[:, y, z, ga])
         + spread("z", wa.at[x, :, z, gb])
@@ -221,25 +255,46 @@
                 t = jnp.tanh(u)
                 half = 0.5 * (1.0 + t)
                 act = (v * half).astype(BF)
-                grad = half + 0.5 * v * (1.0 - t * t) * (
+                deriv = half + 0.5 * v * (1.0 - t * t) * (
                     0.7978845608028654 * (1.0 + 3.0 * 0.044715 * sq)
                 )
-                cols = pl.ds(pl.multiple_of(q * 512 + part * 128, 128), 128)
+                rows = pl.ds(pl.multiple_of(q * 512 + part * 128, 128), 128)
+                cols = pl.ds(pl.multiple_of(part * 128, 128), 128)
                 lo = phase * HALF + c * 128
-                eot[lo : lo + 128, cols] = act.astype(F32).T.astype(BF)
-                slope[phase, c, cols, :] = grad
-
-    @pl.loop(0, 4)
+                et[lo : lo + 128, cols] = act.astype(F32).T
+                slope[phase, c, rows, :] = deriv
+
+    def shift(q):
+        @pl.loop(0, 6)
+        def _(n):
+            rows = pl.ds(pl.multiple_of(n * 128, 128), 128)
+            cols = slice(q * 512, (q + 1) * 512)
+            lane = lax.broadcasted_iota(jnp.int32, (128, 512), 1)
+            edge = lax.broadcasted_iota(jnp.int32, (128, 64), 1)
+            v = et[rows, :]
+            eot[1, rows, cols] = v.astype(BF)
+            eot[0, rows, cols] = jnp.where(lane == 511, 0.0, pltpu.roll(v, 511, 1)).astype(BF)
+            eot[2, rows, cols] = jnp.where(lane == 0, 0.0, pltpu.roll(v, 1, 1)).astype(BF)
+            for j, here, column in ((0, q * 32 + 15, v[:, 0:1]), (2, q * 32 + 16, v[:, 511:512])):
+                old = eot[j, rows, 1024:1088].astype(F32) if q else 0.0
+                eot[j, rows, 1024:1088] = jnp.where(edge == here, column, old).astype(BF)
+
+    @pl.loop(0, 2)
     def _(part):
         activate(0, part)
 
-    for c in gather2:
-        c.wait()
-    gather3 = (
-        spread("z", wa.at[:, :, z, ga])
-        + spread("x", wa.at[x, :, :, gb])
-        + spread("y", wa.at[:, y, :, gc])
-    )
+    settle(gather2)
+    gather3 = [
+        Line("z", lambda c: wa.at[:, :, c, ga]),
+        Line("x", lambda c: wa.at[c, :, :, gb]),
+        Line("y", lambda c: wa.at[:, c, :, gc]),
+    ]
+
+    @pl.loop(2, 4)
+    def _(part):
+        activate(0, part)
+
+    shift(0)
 
     swap_x.wait()
 
@@ -252,6 +307,8 @@
     @pl.loop(0, 4)
     def _(part):
         activate(1, part)
+
+    shift(1)
 
     row_s = lax.broadcasted_iota(jnp.int32, (CIN, HALF), 0)
     col_s = lax.broadcasted_iota(jnp.int32, (CIN, HALF), 1)
@@ -266,41 +323,38 @@
 
     for c in scatter_g:
         c.wait()
-
-    @pl.loop(0, 4)
-    def _(m):
+    swap_g = remote(grad.at[0, :, 0:1024], grad.at[1, :, 0:1024], other_core)
+    swap_g.start()
+
+    for m in range(4):
+        lanes = slice(1024 + m * 128, 1152 + m * 128)
         top, bottom = unpack(tails[2 * m].astype(F32), tails[2 * m + 1].astype(F32))
-        gbuf[0, 8 + m, 0 : EXT // 2, :] = top.astype(BF)
-        gbuf[0, 8 + m, EXT // 2 : EXT, :] = bottom.astype(BF)
-
-    swap_g = remote(gbuf.at[0], gbuf.at[1], other_core)
-    swap_g.start()
-
-    def shifted(q):
-        rows = slice(q * ROWS, (q + 1) * ROWS)
-
-        @pl.loop(0, 12)
-        def _(t):
-            cols = pl.ds(pl.multiple_of(t * 128, 128), 128)
-            shifty[...] = gbuf[q, t].astype(F32)
-            for j in (0, 1, 2):
-                gs[j, rows, cols] = shifty[HALO - 1 + j : HALO - 1 + j + ROWS, :].astype(BF)
-
-    shifted(0)
+        grad[0, 0 : EXT // 2, lanes] = top.astype(BF)
+        grad[0, EXT // 2 : EXT, lanes] = bottom.astype(BF)
+    swap_t = remote(grad.at[0, :, 1024:1536], grad.at[1, :, 1024:1536], other_core)
+    swap_t.start()
     swap_g.wait()
-    shifted(1)
+    swap_t.wait()
 
     scale = 0.5 * float(16 * 8192) ** (-0.5)
 
     def grads(start):
         cols = pl.ds(pl.multiple_of(start, 128), 256)
-        sums = [nn(eot[...], gs[j, :, cols]) * scale for j in (0, 1, 2)]
+        right = jnp.concatenate(
+            [grad[q, HALO : HALO + ROWS, cols] for q in (0, 1)]
+            + [grad[q, lo : lo + HALO, cols] for q in (0, 1) for lo in (0, HALO + ROWS)],
+            axis=0,
+        )
+        sums = [
+            nn(eot[0, :, :1088], right) * scale,
+            nn(eot[1, :, :1024], right[:1024]) * scale,
+            nn(eot[2, :, :1088], right) * scale,
+        ]
         a = [v[:HALF] for v in sums]
         b = [v[HALF:] for v in sums]
         return (a[2] + b[2], a[1] + b[2], a[1] + b[1], a[0] + b[1], a[0] + b[0])
 
-    @pl.loop(0, 4)
-    def _(n):
+    def main_tile(n):
         taps = grads(n * 256)
         for half in (0, 1):
             px = lax.rem(n, 2) * 2 + half
@@ -310,6 +364,80 @@
                     target[k * BLK : (k + 1) * BLK, :] = taps[k][
                         b * BLK : (b + 1) * BLK, half * 128 : (half + 1) * 128
                     ].astype(BF)
+
+    @pl.loop(0, 3)
+    def _(n):
+        main_tile(n)
+
+    relay(gather3)
+    main_tile(3)
+
+    def send_sums(axis, source, slots):
+        copies = []
+        for d in (1, 2, 3):
+            device, c = at(axis, d)
+            copies.append(remote(source(c), slots.at[d - 1], device))
+        for c in copies:
+            c.start()
+        return copies
+
+    def reduce_first(g):
+        ra, rb, rc = [pl.ds(start, size) for start, size in REDUCE[g]]
+        return (
+            send_sums("z", lambda c: wg.at[:, :, c, ra], r1[g][0])
+            + send_sums("x", lambda c: wg.at[c, :, :, rb], r1[g][1])
+            + send_sums("y", lambda c: wg.at[:, c, :, rc], r1[g][2])
+        )
+
+    def reduce_second(g, copies):
+        settle(copies)
+        ra, rb, rc = [pl.ds(start, size) for start, size in REDUCE[g]]
+        (a1, b1, c1), (a2, b2, c2), (a3, b3, c3) = r1[g], s1[g], r2[g]
+        add_up(lambda i, j: wg[i, j, z, ra, :], a1, a2)
+        add_up(lambda i, j: wg[x, i, j, rb, :], b1, b2)
+        add_up(lambda i, j: wg[i, y, j, rc, :], c1, c2)
+        return (
+            send_sums("y", lambda c: a2.at[:, c], a3)
+            + send_sums("z", lambda c: b2.at[:, c], b3)
+            + send_sums("x", lambda c: c2.at[c], c3)
+        )
+
+    def reduce_third(g, copies):
+        settle(copies)
+        (a1, b1, c1), (a2, b2, c2), (a3, b3, c3), (a4, b4, c4) = s1[g], r2[g], s2[g], r3[g]
+        add_up2(lambda i: a1[i, y], a2, a3)
+        add_up2(lambda i: b1[i, z], b2, b3)
+        add_up2(lambda i: c1[x, i], c2, c3)
+        return (
+            send_sums("x", lambda c: a3.at[c], a4)
+            + send_sums("y", lambda c: b3.at[c], b4)
+            + send_sums("z", lambda c: c3.at[c], c4)
+        )
+
+    def reduce_last(g, copies):
+        settle(copies)
+        for (start, size), own, slots in zip(
+            REDUCE[g], (s2[g][0][x], s2[g][1][y], s2[g][2][z]), r3[g]
+        ):
+            fin[start : start + size, :] = own + slots[0] + slots[1] + slots[2]
+
+    def add_up(own, slots, out):
+        @pl.loop(0, 4)
+        def _(i):
+            for j in range(4):
+                total = own(i, j).astype(F32)
+                for d in range(3):
+                    total = total + slots[d, i, j].astype(F32)
+                out[i, j] = total.astype(out.dtype)
+
+    def add_up2(own, slots, out):
+        for i in range(4):
+            total = own(i).astype(F32)
+            for d in range(3):
+                total = total + slots[d, i].astype(F32)
+            out[i] = total
+
+    first0 = reduce_first(0)
 
     @pl.loop(0, 2)
     def _(n):
@@ -333,23 +461,9 @@
                     first[lo:hi, :] = left.astype(BF)
                     second[lo:hi, :] = right.astype(BF)
 
-    def send_sums(axis, source, slots):
-        copies = []
-        for d in (1, 2, 3):
-            device, c = at(axis, d)
-            copies.append(remote(source(c), slots.at[d - 1], device))
-        for c in copies:
-            c.start()
-        return copies
-
-    reduce1 = (
-        send_sums("z", lambda c: wg.at[:, :, c, ga], r1a)
-        + send_sums("x", lambda c: wg.at[c, :, :, gb], r1b)
-        + send_sums("y", lambda c: wg.at[:, c, :, gc], r1c)
-    )
-
-    for c in gather3:
-        c.wait()
+    first1 = reduce_first(1)
+
+    finish(gather3)
 
     @pl.loop(0, 8)
     def _(b):
@@ -377,22 +491,21 @@
     def inputs_back(q):
         @pl.loop(0, 2)
         def _(part):
-            rows = pl.ds(pl.multiple_of(q * 512 + part * 256, 256), 256)
-            middle = gs[1, rows, :]
-            shared = (
-                nt(gs[2, rows, :], wfull[0])
-                + nt(middle, wfull[2])
-                + nt(gs[0, rows, :], wfull[4])
-            )
-            p1[...] = nt(gs[1, rows, :], wfull[1])
-            p3[...] = nt(gs[1, rows, :], wfull[3])
-            after = nt(gs[2, rows, :], wfull[1])
-            before = nt(gs[0, rows, :], wfull[3])
+            block = grad[q, pl.ds(pl.multiple_of(part * 256, 256), TILE), :]
+            for n, k in enumerate((0, 1, 3, 4)):
+                prod[n] = nt(block, wfull[k])
+            middle = block[HALO : HALO + 256]
             skip = nn(
                 jnp.concatenate([middle[:, :512], middle[:, 1024:1280]], axis=1), sel[...]
             )
-            even = shared + p1[...] + before
-            odd_ = shared + after + p3[...]
+            shared = nt(middle, wfull[2])
+            here = slice(HALO, HALO + 256)
+            after = slice(HALO + 1, HALO + 257)
+            before = slice(HALO - 1, HALO + 255)
+            shared = shared + prod[0, after, :] + prod[3, before, :]
+            even = shared + prod[1, here, :] + prod[2, before, :]
+            odd_ = shared + prod[1, after, :] + prod[2, here, :]
+            rows = pl.ds(pl.multiple_of(q * 512 + part * 256, 256), 256)
             for phase, value in ((0, even), (1, odd_)):
                 for c in range(3):
                     lanes = slice(c * 128, (c + 1) * 128)
@@ -409,29 +522,10 @@
 
     swap_d = remote(do, xr2, other_core)
     swap_d.start()
+    second0 = reduce_second(0, first0)
     inputs_back(0)
-
-    for c in reduce1:
-        c.wait()
-
-    def add_up(own, slots, out, lead):
-        @pl.loop(0, lead[0])
-        def _(i):
-            for j in range(lead[1]):
-                total = own(i, j).astype(F32)
-                for d in range(3):
-                    total = total + slots[d, i, j].astype(F32)
-                out[i, j] = total.astype(out.dtype)
-
-    add_up(lambda i, j: wg[i, j, z, ga, :], r1a, s1a, (4, 4))
-    add_up(lambda i, j: wg[x, i, j, gb, :], r1b, s1b, (4, 4))
-    add_up(lambda i, j: wg[i, y, j, gc, :], r1c, s1c, (4, 4))
-    reduce2 = (
-        send_sums("y", lambda c: s1a.at[:, c], r2a)
-        + send_sums("z", lambda c: s1b.at[:, c], r2b)
-        + send_sums("x", lambda c: s1c.at[c], r2c)
-    )
-
+    second1 = reduce_second(1, first1)
+    third0 = reduce_third(0, second0)
     swap_d.wait()
 
     @pl.loop(0, 4)
@@ -442,30 +536,9 @@
         )
         dx_ref[0, rows, :] = nt(both, perm[...]).astype(BF)
 
-    for c in reduce2:
-        c.wait()
-
-    def add_up2(own, slots, out):
-        for i in range(4):
-            total = own(i).astype(F32)
-            for d in range(3):
-                total = total + slots[d, i].astype(F32)
-            out[i] = total
-
-    add_up2(lambda i: s1a[i, y], r2a, s2a)
-    add_up2(lambda i: s1b[i, z], r2b, s2b)
-    add_up2(lambda i: s1c[x, i], r2c, s2c)
-    reduce3 = (
-        send_sums("x", lambda c: s2a.at[c], r3a)
-        + send_sums("y", lambda c: s2b.at[c], r3b)
-        + send_sums("z", lambda c: s2c.at[c], r3c)
-    )
-    for c in reduce3:
-        c.wait()
-    for (start, size), own, slots in zip(
-        PARTS, (s2a[x], s2b[y], s2c[z]), (r3a, r3b, r3c)
-    ):
-        fin[start : start + size, :] = own + slots[0] + slots[1] + slots[2]
+    third1 = reduce_third(1, second1)
+    reduce_last(0, third0)
+    reduce_last(1, third1)
     for k in range(KW):
         wg_ref[k, :, 0:128] = fin[k * BLK : (k + 1) * BLK, :]
 
@@ -484,27 +557,25 @@
 
 
 def on_device(inputs, trunk_grad, weights):
-    sizes = [size for _, size in PARTS]
     vm = pltpu.VMEM
     scratch = [
-        vm((1024, CIN), BF), vm((4096, 192), BF), vm((KW, BLK, 192), BF),
-        vm((4096 + 2 * HALO, 128), BF), vm((8, EXT // 2, 128), BF),
-        vm((2, 12, EXT, 128), BF), vm((8, EXT // 2, 128), BF),
-        vm((3, 2 * ROWS, COUT), BF), vm((EXT, 128), F32),
+        vm((1024, CIN), BF), vm((192, 4096), BF), vm((KW, BLK, 192), BF),
+        vm((4096 + 2 * HALO, 192), BF), vm((8, EXT // 2, 128), BF),
+        vm((2, EXT, COUT), BF), vm((8, EXT // 2, 128), BF),
         vm((CIN, CIN), BF), vm((CIN, HALF), BF),
         vm((2, 3, 1024, 128), F32), vm((1024, HALF), BF), vm((1024, HALF), BF),
         vm((1024, HALF), BF), vm((1024, HALF), BF),
-        vm((CIN, 1024), BF), vm((2, 3, 1024, 128), F32),
+        vm((CIN, 512), F32), vm((3, CIN, 1152), BF), vm((2, 3, 1024, 128), F32),
         vm((4, 4, 4, PIECE, 128), BF), vm((KW, HALF, COUT), BF),
-        vm((4, 4, 4, PIECE, 128), BF),
+        vm((4, 4, 4, PIECE, 128), BF), vm((4, TILE, HALF), F32), vm((PIECE, 128), F32),
     ]
+    sizes = [size for group in REDUCE for _, size in group]
     scratch += [vm((3, 4, 4, n, 128), BF) for n in sizes]
     scratch += [vm((4, 4, n, 128), BF) for n in sizes]
     scratch += [vm((3, 4, n, 128), BF) for n in sizes]
     scratch += [vm((4, n, 128), F32) for n in sizes]
     scratch += [vm((3, n, 128), F32) for n in sizes]
-    scratch += [vm((PIECE, 128), F32), vm((256, HALF), F32), vm((256, HALF), F32)]
-    copies = 27 + 14 + 3 + 27
+    copies = 27 + 14 + 4 + 54
     scratch += [
         pltpu.SemaphoreType.DMA((3,)),
         pltpu.SemaphoreType.DMA((copies,)),
@@ -523,7 +594,7 @@
             collective_id=0, has_side_effects=True, vmem_limit_bytes=63 * 1024 * 1024
         ),
         name="block_backward",
-    )(inputs, trunk_grad, weights)
+    )(inputs, jnp.swapaxes(trunk_grad, 1, 2), weights)
 
 
 def solution(mesh):

time: 111 us -> 103 us (0.928)
  Pallas kernels: 103 us -> 98.5 us
  local copies, waits for them, and re-layouts: 7.25 us -> 3.39 us
    pallas_call x1, Pallas kernels: 103 us -> 98.5 us  [on_device(): pl.pallas_call(kernel, out_shape=(jax.ShapeDtypeStruct((1, 1024, CIN), BF...]
    unnamed x5 -> x4, local copies, waits for them, and re-layouts: 7.25 us -> 3.39 us
where the time goes in v2:
time: 103 us
  Pallas kernels  98.5 us (96%)
  local copies, waits for them, and re-layouts  3.39 us (3%)
    pallas_call x1, Pallas kernels, on_device(): pl.pallas_call(kernel, out_shape=(jax.ShapeDtypeStruct((1, 1024, CIN), BF...  98.5 us
    unnamed x4, local copies, waits for them, and re-layouts  3.39 us

profile of v2, /device:TPU:0, one launch (start us, length us, event | category | flops | bytes accessed | tf_op | source)
XLA Modules:
  0.0 102.5 jit_solution(17003208325201257461)
XLA Ops:
  0.6 98.5 %block_backward.1 = (bf16[1,1024,768]{2,1,0:T(8,128)(2,1)}, f32[5,48,192]{2,1,0:T(8,128)}) custom-call(bf16[1,1024,768]{2,1,0:T(8,128)(2,1)} %x_hbm.1, bf16[1,192,4096]{2,1,0:T(8,128)(2,1)} %bitcast.1, bf16[5,48,192]{2,1,0:T(8,128)(2,1)} %w_hbm.1), custom_call_target="tpu_custom_call" | custom-call | tf_op jit(solution)/shard_map/block_backward/pallas_call | solution.py:584
  99.1 0.0 copy-start
  99.1 2.7 %copy.7 = bf16[1,1024,768]{2,1,0:T(8,128)(2,1)} copy(bf16[1,1024,768]{2,1,0:T(8,128)(2,1)} %get-tuple-element.4) | data formatting | bytes 3145728
  101.8 0.0 copy-done
  101.8 0.7 copy.8
Async XLA Ops:
  99.1 2.7 %copy-start = (f32[5,48,192]{2,1,0:T(8,128)S(1)}, f32[5,48,192]{2,1,0:T(8,128)}, u32[]{:S(2)}) copy-start(f32[5,48,192]{2,1,0:T(8,128)} %get-tuple-element.5) | copy-start | bytes 552964

commit v3 on v2

--- a/solution.py
+++ b/solution.py
@@ -18,8 +18,9 @@
 EXT = ROWS + 2 * HALO
 BLK = 48
 PIECE = 368
-GATHER = ((0, 128), (128, 128), (256, 112))
+GATHER = ((0, 160), (160, 96), (256, 112))
 REDUCE = (((0, 80), (80, 80), (160, 80)), ((240, 48), (288, 48), (336, 32)))
+RELAYED = (True, True)
 TILE = 288
 
 
@@ -207,24 +208,34 @@
 
 
     gather1 = (
-        spread("x", wa.at[x, y, z, ga])
+        spread("y", wa.at[x, y, z, ga])
         + spread("y", wa.at[x, y, z, gb])
-        + spread("z", wa.at[x, y, z, gc])
+        + spread("x", wa.at[x, y, z, gc])
     )
 
-    scatter_g = []
-    for dy in (0, 1):
-        for dx_ in range(4):
-            if dx_ == 0 and dy == 0:
-                continue
+    def scatter(offsets):
+        copies = []
+        for dx_, dy in offsets:
             px, phi = lax.rem(x + dx_, 4), lax.rem(yhi + dy, 2)
             ps = phi * 4 + px
             target = dev(px, phi * 2 + ylo, z, core)
             rows = pl.ds(pl.multiple_of(ps * 512, 512), EXT)
-            scatter_g.append(remote(gpad.at[rows, 0:128], grad.at[0, :, my_lanes], target))
-            scatter_g.append(remote(stail.at[ps], tails.at[s], target))
-    for c in scatter_g:
-        c.start()
+            copies.append(remote(gpad.at[rows, 0:128], grad.at[0, :, my_lanes], target))
+            copies.append(remote(stail.at[ps], tails.at[s], target))
+        for c in copies:
+            c.start()
+        return copies
+
+    scatter_g = scatter(((0, 1),))
+
+    settle(gather1)
+    gather2 = (
+        spread("x", wa.at[x, :, z, ga])
+        + spread("z", wa.at[x, :, z, gb])
+        + spread("z", wa.at[:, y, z, gc])
+    )
+
+    scatter_g += scatter(((1, 1), (3, 1), (2, 1), (2, 0), (1, 0), (3, 0)))
 
     load_x.wait()
 
@@ -239,12 +250,6 @@
     swap_x = remote(xo, xr, other_core)
     swap_x.start()
 
-    settle(gather1)
-    gather2 = (
-        spread("y", wa.at[:, y, z, ga])
-        + spread("z", wa.at[x, :, z, gb])
-        + spread("x", wa.at[x, y, :, gc])
-    )
 
     def activate(q, part):
         for phase in (0, 1):
@@ -283,9 +288,10 @@
     def _(part):
         activate(0, part)
 
-    settle(gather2)
-    gather3 = [
-        Line("z", lambda c: wa.at[:, :, c, ga]),
+    settle(gather2[:3])
+    gather3 = [Line("z", lambda c: wa.at[:, :, c, ga])]
+    settle(gather2[3:])
+    gather3 += [
         Line("x", lambda c: wa.at[c, :, :, gb]),
         Line("y", lambda c: wa.at[:, c, :, gc]),
     ]
@@ -333,6 +339,7 @@
         grad[0, EXT // 2 : EXT, lanes] = bottom.astype(BF)
     swap_t = remote(grad.at[0, :, 1024:1536], grad.at[1, :, 1024:1536], other_core)
     swap_t.start()
+    relay(gather3[:1])
     swap_g.wait()
     swap_t.wait()
 
@@ -369,7 +376,7 @@
     def _(n):
         main_tile(n)
 
-    relay(gather3)
+    relay(gather3[1:])
     main_tile(3)
 
     def send_sums(axis, source, slots):
@@ -381,33 +388,88 @@
             c.start()
         return copies
 
+    class Sum:
+        def __init__(self, axis, block, slots, relayed):
+            self.block, self.slots, self.relayed = block, slots, relayed
+            self.own = {"x": x, "y": y, "z": z}[axis]
+            if not relayed:
+                self.copies = send_sums(axis, lambda c: wg.at[block(c)], slots)
+                return
+            self.onward, self.after = at_ahead(axis, 1)
+            back, before = at_ahead(axis, -1)
+            _, far = at_ahead(axis, 2)
+            self.first = remote(wg.at[block(far)], slots.at[0], self.onward)
+            self.second = remote(wg.at[block(before)], slots.at[1], back)
+            self.first.start()
+            self.second.start()
+
+        def total(self, c, i, j, terms):
+            lead = [i, j]
+            block = self.block(c)
+            place = tuple(lead.pop(0) if isinstance(n, slice) else n for n in block[:3])
+            value = wg[place + block[3:]].astype(F32)
+            for d in terms:
+                value = value + self.slots[d, i, j].astype(F32)
+            return value
+
+        def owned(self, i, j):
+            return self.total(self.own, i, j, (1, 2) if self.relayed else (0, 1, 2))
+
+        def relay(self):
+            if not self.relayed:
+                return
+            self.first.wait_recv()
+            slots = self.slots
+
+            @pl.loop(0, 4)
+            def _(i):
+                for j in range(4):
+                    slots[0, i, j] = self.total(self.after, i, j, (0,)).astype(BF)
+
+            self.third = remote(slots.at[0], slots.at[2], self.onward)
+            self.third.start()
+
+        def finish(self, out):
+            if self.relayed:
+                self.first.wait_send()
+                self.second.wait()
+                self.third.wait()
+            else:
+                settle(self.copies)
+
+            @pl.loop(0, 4)
+            def _(i):
+                for j in range(4):
+                    out[i, j] = self.owned(i, j).astype(BF)
+
+    every = slice(None)
+
     def reduce_first(g):
         ra, rb, rc = [pl.ds(start, size) for start, size in REDUCE[g]]
-        return (
-            send_sums("z", lambda c: wg.at[:, :, c, ra], r1[g][0])
-            + send_sums("x", lambda c: wg.at[c, :, :, rb], r1[g][1])
-            + send_sums("y", lambda c: wg.at[:, c, :, rc], r1[g][2])
-        )
-
-    def reduce_second(g, copies):
+        return [
+            Sum("z", lambda c: (every, every, c, ra), r1[g][0], RELAYED[g]),
+            Sum("x", lambda c: (c, every, every, rb), r1[g][1], RELAYED[g]),
+            Sum("y", lambda c: (every, c, every, rc), r1[g][2], RELAYED[g]),
+        ]
+
+    def reduce_second(g, lines):
+        copies = []
+        for n, (line, out, slots) in enumerate(zip(lines, s1[g], r2[g])):
+            line.finish(out)
+            if n == 0:
+                copies += send_sums("y", lambda c: out.at[:, c], slots)
+            elif n == 1:
+                copies += send_sums("z", lambda c: out.at[:, c], slots)
+            else:
+                copies += send_sums("x", lambda c: out.at[c], slots)
+        return copies
+
+    def reduce_third(g, lines, copies):
         settle(copies)
-        ra, rb, rc = [pl.ds(start, size) for start, size in REDUCE[g]]
-        (a1, b1, c1), (a2, b2, c2), (a3, b3, c3) = r1[g], s1[g], r2[g]
-        add_up(lambda i, j: wg[i, j, z, ra, :], a1, a2)
-        add_up(lambda i, j: wg[x, i, j, rb, :], b1, b2)
-        add_up(lambda i, j: wg[i, y, j, rc, :], c1, c2)
-        return (
-            send_sums("y", lambda c: a2.at[:, c], a3)
-            + send_sums("z", lambda c: b2.at[:, c], b3)
-            + send_sums("x", lambda c: c2.at[c], c3)
-        )
-
-    def reduce_third(g, copies):
-        settle(copies)
-        (a1, b1, c1), (a2, b2, c2), (a3, b3, c3), (a4, b4, c4) = s1[g], r2[g], s2[g], r3[g]
-        add_up2(lambda i: a1[i, y], a2, a3)
-        add_up2(lambda i: b1[i, z], b2, b3)
-        add_up2(lambda i: c1[x, i], c2, c3)
+        (a2, b2, c2), (a3, b3, c3), (a4, b4, c4) = r2[g], s2[g], r3[g]
+        add_up2(lambda i: lines[0].owned(i, y), a2, a3)
+        add_up2(lambda i: lines[1].owned(i, z), b2, b3)
+        add_up2(lambda i: lines[2].owned(x, i), c2, c3)
         return (
             send_sums("x", lambda c: a3.at[c], a4)
             + send_sums("y", lambda c: b3.at[c], b4)
@@ -421,18 +483,9 @@
         ):
             fin[start : start + size, :] = own + slots[0] + slots[1] + slots[2]
 
-    def add_up(own, slots, out):
-        @pl.loop(0, 4)
-        def _(i):
-            for j in range(4):
-                total = own(i, j).astype(F32)
-                for d in range(3):
-                    total = total + slots[d, i, j].astype(F32)
-                out[i, j] = total.astype(out.dtype)
-
     def add_up2(own, slots, out):
         for i in range(4):
-            total = own(i).astype(F32)
+            total = own(i)
             for d in range(3):
                 total = total + slots[d, i].astype(F32)
             out[i] = total
@@ -522,10 +575,12 @@
 
     swap_d = remote(do, xr2, other_core)
     swap_d.start()
+    relay(first0)
+    relay(first1)
+    inputs_back(0)
     second0 = reduce_second(0, first0)
-    inputs_back(0)
     second1 = reduce_second(1, first1)
-    third0 = reduce_third(0, second0)
+    third0 = reduce_third(0, first0, second0)
     swap_d.wait()
 
     @pl.loop(0, 4)
@@ -536,7 +591,7 @@
         )
         dx_ref[0, rows, :] = nt(both, perm[...]).astype(BF)
 
-    third1 = reduce_third(1, second1)
+    third1 = reduce_third(1, first1, second1)
     reduce_last(0, third0)
     reduce_last(1, third1)
     for k in range(KW):

time: 103 us -> 96.6 us (0.938)
  Pallas kernels: 98.5 us -> 92.4 us
    pallas_call x1, Pallas kernels: 98.5 us -> 92.4 us  [on_device(): pl.pallas_call(kernel, out_shape=(jax.ShapeDtypeStruct((1, 1024, CIN), BF...]
where the time goes in v3:
time: 96.6 us; the launch traced here: 96.4 us
  Pallas kernels  92.4 us (96%)
  local copies, waits for them, and re-layouts  3.39 us (4%)
    pallas_call x1, Pallas kernels, on_device(): pl.pallas_call(kernel, out_shape=(jax.ShapeDtypeStruct((1, 1024, CIN), BF...  92.4 us
    unnamed x4, local copies, waits for them, and re-layouts  3.39 us

profile of v3, /device:TPU:0, one launch (start us, length us, event | category | flops | bytes accessed | tf_op | source)
XLA Modules:
  0.0 96.4 jit_solution(17297738121931568397)
XLA Ops:
  0.6 92.4 %block_backward.1 = (bf16[1,1024,768]{2,1,0:T(8,128)(2,1)}, f32[5,48,192]{2,1,0:T(8,128)}) custom-call(bf16[1,1024,768]{2,1,0:T(8,128)(2,1)} %x_hbm.1, bf16[1,192,4096]{2,1,0:T(8,128)(2,1)} %bitcast.1, bf16[5,48,192]{2,1,0:T(8,128)(2,1)} %w_hbm.1), custom_call_target="tpu_custom_call" | custom-call | tf_op jit(solution)/shard_map/block_backward/pallas_call | solution.py:639
  93.0 0.0 copy-start
  93.1 2.7 %copy.7 = bf16[1,1024,768]{2,1,0:T(8,128)(2,1)} copy(bf16[1,1024,768]{2,1,0:T(8,128)(2,1)} %get-tuple-element.4) | data formatting | bytes 3145728
  95.7 0.0 copy-done
  95.7 0.7 copy.8
Async XLA Ops:
  93.0 2.7 %copy-start = (f32[5,48,192]{2,1,0:T(8,128)S(1)}, f32[5,48,192]{2,1,0:T(8,128)}, u32[]{:S(2)}) copy-start(f32[5,48,192]{2,1,0:T(8,128)} %get-tuple-element.5) | copy-start | bytes 552964

commit v4 on v3

--- a/solution.py
+++ b/solution.py
@@ -21,7 +21,6 @@
 GATHER = ((0, 160), (160, 96), (256, 112))
 REDUCE = (((0, 80), (80, 80), (160, 80)), ((240, 48), (288, 48), (336, 32)))
 RELAYED = (True, True)
-TILE = 288
 
 
 def nt(left, right):
@@ -372,12 +371,16 @@
                         b * BLK : (b + 1) * BLK, half * 128 : (half + 1) * 128
                     ].astype(BF)
 
-    @pl.loop(0, 3)
+    @pl.loop(0, 1)
     def _(n):
         main_tile(n)
 
     relay(gather3[1:])
-    main_tile(3)
+
+    @pl.loop(1, 4)
+    def _(n):
+        main_tile(n)
+
 
     def send_sums(axis, source, slots):
         copies = []
@@ -542,23 +545,23 @@
             wfull[4, pl.ds(pl.multiple_of(base + 32, 16), 16), lanes] = two[:16].astype(BF)
 
     def inputs_back(q):
-        @pl.loop(0, 2)
-        def _(part):
-            block = grad[q, pl.ds(pl.multiple_of(part * 256, 256), TILE), :]
-            for n, k in enumerate((0, 1, 3, 4)):
-                prod[n] = nt(block, wfull[k])
-            middle = block[HALO : HALO + 256]
+        for n, k in enumerate((0, 1, 3, 4, 2)):
+            prod[n] = nt(grad[q], wfull[k])
+
+        for part in (0, 1):
+            rows = pl.ds(pl.multiple_of(q * 512 + part * 256, 256), 256)
+            middle = grad[q, pl.ds(pl.multiple_of(part * 256 + HALO, 16), 256), :]
             skip = nn(
                 jnp.concatenate([middle[:, :512], middle[:, 1024:1280]], axis=1), sel[...]
             )
-            shared = nt(middle, wfull[2])
-            here = slice(HALO, HALO + 256)
-            after = slice(HALO + 1, HALO + 257)
-            before = slice(HALO - 1, HALO + 255)
-            shared = shared + prod[0, after, :] + prod[3, before, :]
-            even = shared + prod[1, here, :] + prod[2, before, :]
-            odd_ = shared + prod[1, after, :] + prod[2, here, :]
-            rows = pl.ds(pl.multiple_of(q * 512 + part * 256, 256), 256)
+
+            def shifted(n, by, part=part):
+                start = part * 256 + HALO + by
+                return prod[n, start : start + 256, :]
+
+            shared = shifted(4, 0) + shifted(0, 1) + shifted(3, -1)
+            even = shared + shifted(1, 0) + shifted(2, -1)
+            odd_ = shared + shifted(1, 1) + shifted(2, 0)
             for phase, value in ((0, even), (1, odd_)):
                 for c in range(3):
                     lanes = slice(c * 128, (c + 1) * 128)
@@ -622,7 +625,7 @@
         vm((1024, HALF), BF), vm((1024, HALF), BF),
         vm((CIN, 512), F32), vm((3, CIN, 1152), BF), vm((2, 3, 1024, 128), F32),
         vm((4, 4, 4, PIECE, 128), BF), vm((KW, HALF, COUT), BF),
-        vm((4, 4, 4, PIECE, 128), BF), vm((4, TILE, HALF), F32), vm((PIECE, 128), F32),
+        vm((4, 4, 4, PIECE, 128), BF), vm((5, EXT, HALF), F32), vm((PIECE, 128), F32),
     ]
     sizes = [size for group in REDUCE for _, size in group]
     scratch += [vm((3, 4, 4, n, 128), BF) for n in sizes]

time: 96.6 us -> 93.9 us (0.972)
  Pallas kernels: 92.4 us -> 89.8 us
    pallas_call x1, Pallas kernels: 92.4 us -> 89.8 us  [on_device(): pl.pallas_call(kernel, out_shape=(jax.ShapeDtypeStruct((1, 1024, CIN), BF...]
where the time goes in v4:
time: 93.9 us; the launch traced here: 93.8 us
  Pallas kernels  89.8 us (96%)
  local copies, waits for them, and re-layouts  3.39 us (4%)
    pallas_call x1, Pallas kernels, on_device(): pl.pallas_call(kernel, out_shape=(jax.ShapeDtypeStruct((1, 1024, CIN), BF...  89.8 us
    unnamed x4, local copies, waits for them, and re-layouts  3.39 us

profile of v4, /device:TPU:0, one launch (start us, length us, event | category | flops | bytes accessed | tf_op | source)
XLA Modules:
  0.0 93.8 jit_solution(51565231679647721)
XLA Ops:
  0.6 89.8 %block_backward.1 = (bf16[1,1024,768]{2,1,0:T(8,128)(2,1)}, f32[5,48,192]{2,1,0:T(8,128)}) custom-call(bf16[1,1024,768]{2,1,0:T(8,128)(2,1)} %x_hbm.1, bf16[1,192,4096]{2,1,0:T(8,128)(2,1)} %bitcast.1, bf16[5,48,192]{2,1,0:T(8,128)(2,1)} %w_hbm.1), custom_call_target="tpu_custom_call" | custom-call | tf_op jit(solution)/shard_map/block_backward/pallas_call | solution.py:642
  90.4 0.0 copy-start
  90.4 2.7 %copy.7 = bf16[1,1024,768]{2,1,0:T(8,128)(2,1)} copy(bf16[1,1024,768]{2,1,0:T(8,128)(2,1)} %get-tuple-element.4) | data formatting | bytes 3145728
  93.1 0.0 copy-done
  93.1 0.7 copy.8
Async XLA Ops:
  90.4 2.7 %copy-start = (f32[5,48,192]{2,1,0:T(8,128)S(1)}, f32[5,48,192]{2,1,0:T(8,128)}, u32[]{:S(2)}) copy-start(f32[5,48,192]{2,1,0:T(8,128)} %get-tuple-element.5) | copy-start | bytes 552964
